TPU v7x, 32 devices: a whole 2x2x4 slice. The times are simulated.
32 devices in a mesh: row: 8 (over y, x, core), head: 4 (over z).
Axes of the slice: x: 2, y: 2, z: 4, core: 2. Of those that a mesh axis runs over, the one named last changes fastest.
Arguments:
- features: bfloat16 [4096, 1024], P('row'), may hold values from -6 to 6
- w_qkv: bfloat16 [3, 1024, 1024], P(None, None, 'head'), may hold values from -0.1875 to 0.1875
- w_out: bfloat16 [1024, 1024], P('head'), may hold values from -0.1875 to 0.1875
- bias_gain: float32 [16], P('head'), may hold values from 0.5 to 1.5
- edge_bias: bfloat16 [64, 64, 4096], P('row'), may hold values from -6 to 250
- neighbours: int32 [64, 64], P('row'), may hold values from 0 to 63, as said below
- counts: int32 [64], P('row'), may hold values from 1 to 64, as said below
Outputs:
- mixed: bfloat16 [4096, 1024], P('row', 'head')
Inputs may be any that keep to these rules, and one draw needn't show every extreme that they name: `neighbours`: key block b is owned by row device b // 8. Over all slots of the query blocks of one row device, at most 2 distinct key blocks of any one owner are named, and for every row device some owner has exactly 2. `counts`: the first query block of every row device has all 64 slots live.
All inputs are finite; a program needn't handle non-finite values.
Results may differ from a plain program's by a relative error of at most 0.011.
Values may be sent and summed in bfloat16 or wider, within the bound.
A program may use at most 256 MiB of HBM per device.

v0:
```python
import jax
import jax.numpy as jnp
from jax import lax
from jax.sharding import PartitionSpec as P

HD = 64
BLK = 64
NB = 64


def body(features, w_qkv, w_out, bias_gain, edge_bias, neighbours, counts):
    rows = features.shape[0]
    width_heads = w_qkv.shape[2]
    heads_dev = width_heads // HD
    blocks_dev = rows // BLK
    row_devs = lax.axis_size("row")
    projected = jnp.einsum(
        "rd,tdc->trc", features, w_qkv, preferred_element_type=jnp.float32
    ).astype(jnp.bfloat16)
    queries = projected[0]
    kv_heads = projected[1:].reshape(2, rows, heads_dev, HD).transpose(0, 2, 1, 3)
    gathered = lax.all_gather(kv_heads, "row", axis=2, tiled=True)
    key_table = gathered.reshape(2, heads_dev, row_devs * blocks_dev, BLK, HD)
    group_size = min(8, blocks_dev)
    groups = blocks_dev // group_size
    scale = HD ** (-0.5)
    span = NB * BLK
    query_groups = queries.reshape(groups, group_size, BLK, heads_dev, HD).transpose(0, 3, 1, 2, 4)
    index_groups = neighbours.reshape(groups, group_size, NB)
    bias_groups = edge_bias.reshape(groups, group_size, BLK, span)
    count_groups = counts.reshape(groups, group_size)
    column_slot = jnp.arange(span, dtype=jnp.int32) // BLK

    def attend(inputs):
        query_tile, slot_ids, bias_tile, live_count = inputs
        near_keys = key_table[0][:, slot_ids].reshape(heads_dev, group_size, span, HD)
        near_values = key_table[1][:, slot_ids].reshape(heads_dev, group_size, span, HD)
        score = (
            jnp.einsum("hgqd,hgmd->hgqm", query_tile, near_keys, preferred_element_type=jnp.float32)
            * scale
        )
        score = score + bias_gain[:, None, None, None] * bias_tile.astype(jnp.float32)[None]
        live = column_slot[None, :] < live_count[:, None]
        score = jnp.where(live[None, :, None, :], score, jnp.float32(-1e30))
        top = jnp.max(score, axis=3, keepdims=True)
        expo = jnp.exp(score - top)
        total = jnp.sum(expo, axis=3, keepdims=True)
        weights = (expo / total).astype(jnp.bfloat16)
        result = jnp.einsum(
            "hgqm,hgmd->hgqd", weights, near_values, preferred_element_type=jnp.float32
        )
        return result.astype(jnp.bfloat16)

    attended = lax.map(attend, (query_groups, index_groups, bias_groups, count_groups))
    attended = attended.transpose(1, 0, 2, 3, 4).reshape(heads_dev, rows, HD)
    weight_heads = w_out.reshape(heads_dev, HD, w_out.shape[1])
    partial_out = jnp.einsum(
        "hrd,hdo->ro", attended, weight_heads, preferred_element_type=jnp.float32
    )
    return lax.psum_scatter(partial_out, "head", scatter_dimension=1, tiled=True).astype(
        jnp.bfloat16
    )


def solution(mesh):
    in_specs = (
        P("row", None),
        P(None, None, "head"),
        P("head", None),
        P("head"),
        P("row", None, None),
        P("row", None),
        P("row"),
    )
    out_specs = P("row", "head")
    return jax.shard_map(body, mesh=mesh, in_specs=in_specs, out_specs=out_specs, check_vma=False)
```

profile of v0, /device:TPU:0, one launch (start us, length us, event | category | flops | bytes accessed | tf_op | source)
XLA Modules:
  0.0 376.3 jit_solution(6359873151709441695)
XLA Ops:
  6.5 1.4 copy-done
  7.9 2.2 fusion.10
  10.2 0.9 slice.25
  11.2 0.7 compare_select_fusion
  11.8 0.1 reshape.81
  11.9 0.3 reshape_squeeze.3
  12.2 0.4 copy.19
  12.6 6.6 %convert_element_type.25 = f32[8,64,4096]{2,1,0:T(8,128)} convert(bf16[8,64,4096]{2,1,0:T(8,128)(2,1)} %param.11) | non-fusion elementwise | flops 2097152 | bytes 12582912 | tf_op jit(solution)/shard_map/while/body/eval_jaxpr/convert_element_type | solution.py:42
  19.2 0.1 broadcast_compare_fusion
  19.3 32.1 %all-gather.2.cloned.1.call-done = bf16[2,4,4096,64]{2,3,1,0:T(8,128)(2,1)} async-done(((bf16[2,4,512,64]{2,3,1,0:T(8,128)(2,1)}), bf16[2,4,4096,64]{2,3,1,0:T(8,128)(2,1)}) %all-gather.2.cloned.1.call-update) | async-done | bytes 4194320 | tf_op jit(solution)/shard_map/all_gather | solution.py:22
  51.4 4.8 %fusion.25 = (bf16[1,4,4096,64]{2,3,1,0:T(8,128)(2,1)}, bf16[1,4,4096,64]{2,3,1,0:T(8,128)(2,1)}) fusion(bf16[2,4,4096,64]{2,3,1,0:T(8,128)(2,1)} %all-gather.2.cloned.1.call-done), kind=kLoop, calls=%fused_computation.34 | loop fusion | bytes 8388608 | tf_op jit(solution)/shard_map/while/body/eval_jaxpr/slice | solution.py:36
  56.2 4.8 %copy.20 = bf16[1,4,4096,64]{3,2,1,0:T(8,128)(2,1)} copy(bf16[1,4,4096,64]{2,3,1,0:T(8,128)(2,1)} %get-tuple-element.21) | data formatting | bytes 4194304 | tf_op jit(solution)/shard_map/while/body/eval_jaxpr/slice | solution.py:36
  60.9 4.8 %copy.23 = bf16[1,4,4096,64]{3,2,1,0:T(8,128)(2,1)} copy(bf16[1,4,4096,64]{2,3,1,0:T(8,128)(2,1)} %get-tuple-element.22) | data formatting | bytes 4194304 | tf_op jit(solution)/shard_map/while/body/eval_jaxpr/slice | solution.py:37
  65.7 18.2 %gather_fusion.1 = bf16[512,4,64,64]{3,2,1,0:T(8,128)(2,1)} fusion(bf16[4,64,64,64]{3,2,1,0:T(8,128)(2,1)} %bitcast.54, s32[1024]{0:T(1024)S(1)} %pad_clamp_fusion), kind=kCustom, calls=%fused_computation.1 | custom fusion | bytes 33556480 | tf_op jit(solution)/shard_map/while/body/eval_jaxpr/gather | solution.py:37
  83.9 44.5 %copy.25 = bf16[4,8,64,64,64]{3,2,4,1,0:T(8,128)(2,1)} copy(bf16[4,8,64,64,64]{4,3,0,2,1:T(8,128)(2,1)} %bitcast.56) | data formatting | bytes 33554432 | tf_op jit(solution)/shard_map/while/body/eval_jaxpr/gather | solution.py:37
  128.4 44.1 %reshape.77 = bf16[4,8,4096,64]{2,3,1,0:T(8,128)(2,1)} reshape(bf16[4,8,64,64,64]{3,2,4,1,0:T(8,128)(2,1)} %copy.25) | data formatting | bytes 33554432 | tf_op jit(solution)/shard_map/while/body/eval_jaxpr/reshape | solution.py:37
  172.4 18.2 %gather_fusion = bf16[512,4,64,64]{3,2,1,0:T(8,128)(2,1)} fusion(bf16[4,64,64,64]{3,2,1,0:T(8,128)(2,1)} %bitcast.53, s32[1024]{0:T(1024)S(1)} %pad_clamp_fusion), kind=kCustom, calls=%fused_computation | custom fusion | bytes 33556480 | tf_op jit(solution)/shard_map/while/body/eval_jaxpr/gather | solution.py:36
  190.6 44.5 %copy.22 = bf16[4,8,64,64,64]{3,2,4,1,0:T(8,128)(2,1)} copy(bf16[4,8,64,64,64]{4,3,0,2,1:T(8,128)(2,1)} %bitcast.55) | data formatting | bytes 33554432 | tf_op jit(solution)/shard_map/while/body/eval_jaxpr/gather | solution.py:36
  235.1 44.1 %reshape.76 = bf16[4,8,4096,64]{2,3,1,0:T(8,128)(2,1)} reshape(bf16[4,8,64,64,64]{3,2,4,1,0:T(8,128)(2,1)} %copy.22) | data formatting | bytes 33554432 | tf_op jit(solution)/shard_map/while/body/eval_jaxpr/reshape | solution.py:36
  279.2 24.4 %fusion.26 = (f32[4,8,64]{2,1,0:T(8,128)S(1)}, f32[4,8,64,4096]{3,2,1,0:T(8,128)}) fusion(f32[8,64,4096]{2,1,0:T(8,128)} %convert_element_type.25, f32[4]{0:T(128)S(1)} %copy-done.3, pred[8,4096]{1,0:T(8,128)(4,1)S(1)} %broadcast_compare_fusion, bf16[4,8,4096,64]{2,3,1,0:T(8,128)(2,1)} %reshape.76, bf16[1,8,64,4,64]{4,2,1,3,0:T(8,128)(2,1)S(1)} %copy.19), kind=kOutput, calls=%fused_computation.35 | convolution fusion | flops 1124077568 | bytes 59023376 | tf_op jit(solution)/shard_map/while/body/eval_jaxpr/sub | solution.py:46
  303.6 18.2 %fusion.11 = bf16[4,8,64,64]{3,2,1,0:T(8,128)(2,1)S(1)} fusion(bf16[4,8,4096,64]{2,3,1,0:T(8,128)(2,1)} %reshape.77, f32[4,8,64,4096]{3,2,1,0:T(8,128)} %get-tuple-element.24, f32[4,8,64]{2,1,0:T(8,128)S(1)} %get-tuple-element.23), kind=kOutput, calls=%fused_computation.17 | convolution fusion | flops 1090650112 | bytes 50601984 | tf_op jit(solution)/shard_map/while/body/eval_jaxpr/hgqm,hgmd->hgqd/dot_general | solution.py:49
  321.8 1.8 convolution_bitcast_fusion
  323.6 44.1 %reduce-scatter.2.cloned.1.call-done = f32[512,256]{1,0:T(8,128)} async-done(((f32[512,1024]{1,0:T(8,128)}), f32[512,256]{1,0:T(8,128)}) %reduce-scatter.2.cloned.1.call-update) | async-done | bytes 524304 | tf_op jit(solution)/shard_map/reduce_scatter | solution.py:60
  367.7 1.8 convert_element_type.28
  (16 shorter events, 0.1 us)
Async XLA Ops:
  6.5 1.4 copy-start
  6.5 12.7 %copy-start.4 = (s32[8]{0:T(128)S(1)}, s32[8]{0:T(128)}, u32[]{:S(2)}) copy-start(s32[8]{0:T(128)} %param.13) | copy-start | bytes 100
  6.5 44.8 %all-gather.2.cloned.1.call-start = ((), (), s32[]{:S(2)}) async-start(), calls=%async_computation.1 | async-start | bytes 4718592 | tf_op jit(solution)/shard_map/all_gather | solution.py:22
  11.1 356.7 %reduce-scatter.2.cloned.1.call-start = ((), (), s32[]{:S(2)}) async-start(), calls=%async_computation.2 | async-start | bytes 2621440 | tf_op jit(solution)/shard_map/reduce_scatter | solution.py:60
  235.1 44.1 %copy-start.3 = (f32[4]{0:T(128)S(1)}, f32[4]{0:T(128)}, u32[]{:S(2)}) copy-start(f32[4]{0:T(128)} %param.10) | copy-start | bytes 52
  303.6 18.2 %copy-start.2 = (bf16[256,1024]{1,0:T(8,128)(2,1)S(1)}, bf16[256,1024]{1,0:T(8,128)(2,1)}, u32[]{:S(2)}) copy-start(bf16[256,1024]{1,0:T(8,128)(2,1)} %param.9) | copy-start | bytes 1572868
  303.6 65.9 %copy-start.1 = (bf16[3,1024,256]{2,1,0:T(8,128)(2,1)S(1)}, bf16[3,1024,256]{2,1,0:T(8,128)(2,1)}, u32[]{:S(2)}) copy-start(bf16[3,1024,256]{2,1,0:T(8,128)(2,1)} %param.8) | copy-start | bytes 4718596
Sparse Core Ops, SparseCore 0:
  11.2 40.1 all-gather.1
  323.8 43.9 reduce-scatter.1
where the time goes:
time: 381 us; the launch traced here: 376 us
  local copies, waits for them, and re-layouts  231 us (61%)
  waiting for transfers between devices  76.2 us (20%)
  matrix products  46.7 us (12%)
  between operations  13.5 us (4%)
  other arithmetic  9.14 us (2%)
    gather x2, local copies, waits for them, and re-layouts, attend(): key_table[1][:, slot_ids].reshape(heads_dev, group_size, span, HD)  62.6 us
    gather x2, local copies, waits for them, and re-layouts, attend(): key_table[0][:, slot_ids].reshape(heads_dev, group_size, span, HD)  62.6 us
    reduce_scatter x1, waiting for transfers between devices, body(): lax.psum_scatter(partial_out, 'head', scatter_dimension=1, tiled=True)  44.1 us
    reshape x1, local copies, waits for them, and re-layouts, attend(): key_table[1][:, slot_ids].reshape(heads_dev, group_size, span, HD)  44.1 us
    reshape x1, local copies, waits for them, and re-layouts, attend(): key_table[0][:, slot_ids].reshape(heads_dev, group_size, span, HD)  44.1 us
    all_gather x1, waiting for transfers between devices, body(): gathered = lax.all_gather(kv_heads, 'row', axis=2, tiled=True)  32.1 us
    sub x1, matrix products, attend(): expo = jnp.exp(score - top)  24.4 us
    dot_general x1, matrix products, attend(): jnp.einsum('hgqm,hgmd->hgqd', weights, near_values, preferred_element_typ...  18.2 us
  transfers between devices with their start and end apart: 2, of which 2 were waited for; matrix products, arithmetic and copies ran while one was open for 2% of the time, Pallas kernels for 0%

commit v1 on v0

v1 whole, which is shorter than its diff:
```python
import functools

import jax
import jax.numpy as jnp
from jax import lax
from jax.experimental import pallas as pl
from jax.experimental.pallas import tpu as pltpu
from jax.sharding import PartitionSpec as P

HD = 64
BLK = 64
NB = 64
HALF = BLK // 2
CAP = 2
NEG = -1e30
LOG2E = 1.4426950408889634


def swap_halves(x):
    return pltpu.roll(x, HD, 1)


def project_kernel(row_devs, req_ref, x_ref, w_ref, q_ref, *rest):
    sends, kv = rest[:row_devs], rest[row_devs]
    rows, width = kv.shape[0], w_ref.shape[2]
    x = x_ref[...]
    q = jnp.dot(x, w_ref[0], preferred_element_type=jnp.float32)
    for t in range(2):
        kv[:, t * width : (t + 1) * width] = jnp.dot(
            x, w_ref[1 + t], preferred_element_type=jnp.float32
        ).astype(jnp.bfloat16)
    q = q.reshape(rows // BLK, 2, HALF, width)
    top = q[:, 0].reshape(rows // 2, width)
    bottom = q[:, 1].reshape(rows // 2, width)
    first = lax.broadcasted_iota(jnp.int32, (rows // 2, 2 * HD), 1) < HD
    for pair in range(width // (2 * HD)):
        a = top[:, pair * 2 * HD : (pair + 1) * 2 * HD]
        b = bottom[:, pair * 2 * HD : (pair + 1) * 2 * HD]
        q_ref[2 * pair] = jnp.where(first, a, swap_halves(b)).astype(jnp.bfloat16)
        q_ref[2 * pair + 1] = jnp.where(first, swap_halves(a), b).astype(jnp.bfloat16)
    for s in range(row_devs):
        for c in range(CAP):
            at = pl.multiple_of(req_ref[s, c] * BLK, BLK)
            sends[s][c * BLK : (c + 1) * BLK, :] = kv[pl.ds(at, BLK), :]


def project(features, w_qkv, requests, row_devs):
    rows = features.shape[0]
    width = w_qkv.shape[2]
    out = [jax.ShapeDtypeStruct((width // HD, rows // 2, 2 * HD), jnp.bfloat16)]
    out += [jax.ShapeDtypeStruct((CAP * BLK, 2 * width), jnp.bfloat16)] * row_devs
    vmem = pl.BlockSpec(memory_space=pltpu.VMEM)
    return pl.pallas_call(
        functools.partial(project_kernel, row_devs),
        out_shape=out,
        in_specs=[pl.BlockSpec(memory_space=pltpu.SMEM), vmem, vmem],
        out_specs=[vmem] * len(out),
        scratch_shapes=[pltpu.VMEM((rows, 2 * width), jnp.bfloat16)],
        compiler_params=pltpu.CompilerParams(vmem_limit_bytes=40 * 2**20),
        name="project",
    )(requests, features, w_qkv)


def sums_kernel(heads, units, umap_ref, count_ref, gain_ref, bias_ref, t_ref, m_ref, tiles, best, acc):
    g = pl.program_id(0)
    count = count_ref[g]
    best[...] = jnp.full(best.shape, NEG, jnp.float32)
    acc[...] = jnp.zeros(acc.shape, jnp.float32)
    first = lax.broadcasted_iota(jnp.int32, (HALF, 2 * BLK), 1) < BLK

    def arrange(i, carry):
        for step in range(2):
            pair = i * 2 + step
            at = pl.multiple_of(pair * 2 * BLK, 2 * BLK)
            a = bias_ref[0, 0:HALF, pl.ds(at, 2 * BLK)].astype(jnp.float32)
            b = bias_ref[0, HALF:BLK, pl.ds(at, 2 * BLK)].astype(jnp.float32)
            for odd in range(2):
                j = 2 * pair + odd
                tile = jnp.where(first, swap_halves(a), b) if odd else jnp.where(first, a, swap_halves(b))
                tile = jnp.where(j < count, tile, NEG)
                tiles[j] = tile
                u = umap_ref[g, j]
                best[u] = jnp.maximum(best[u], tile)
        return carry

    lax.fori_loop(0, NB // 4, arrange, 0)
    gains = [gain_ref[h] * LOG2E for h in range(heads)]

    def add(i, carry):
        for step in range(4):
            j = i * 4 + step
            u = umap_ref[g, j]
            d = tiles[j] - best[u]
            e = [jnp.exp2(d * gains[h]) for h in range(heads)]
            for h in range(heads):
                acc[u, h] += e[h]
        return carry

    lax.fori_loop(0, (count + 3) // 4, add, 0)
    for u in range(units):
        m_ref[:, u * 2 * BLK : (u + 1) * 2 * BLK] = best[u].astype(jnp.bfloat16)
        for h in range(heads):
            t_ref[h, :, u * 2 * BLK : (u + 1) * 2 * BLK] = acc[u, h].astype(jnp.bfloat16)


def sums(umap, counts, bias_gain, edge_bias, units):
    blocks = umap.shape[0]
    heads = bias_gain.shape[0]
    wide = units * 2 * BLK
    rows2 = blocks * HALF
    grid_spec = pltpu.PrefetchScalarGridSpec(
        num_scalar_prefetch=3,
        grid=(blocks,),
        in_specs=[pl.BlockSpec((1, BLK, NB * BLK), lambda g, *_: (g, 0, 0))],
        out_specs=[
            pl.BlockSpec((heads, HALF, wide), lambda g, *_: (0, g, 0)),
            pl.BlockSpec((HALF, wide), lambda g, *_: (g, 0)),
        ],
        scratch_shapes=[
            pltpu.VMEM((NB, HALF, 2 * BLK), jnp.float32),
            pltpu.VMEM((units, HALF, 2 * BLK), jnp.float32),
            pltpu.VMEM((units, heads, HALF, 2 * BLK), jnp.float32),
        ],
    )
    return pl.pallas_call(
        functools.partial(sums_kernel, heads, units),
        out_shape=[
            jax.ShapeDtypeStruct((heads, rows2, wide), jnp.bfloat16),
            jax.ShapeDtypeStruct((rows2, wide), jnp.bfloat16),
        ],
        grid_spec=grid_spec,
        compiler_params=pltpu.CompilerParams(vmem_limit_bytes=40 * 2**20),
        cost_estimate=pl.CostEstimate(
            flops=10 * blocks * heads * BLK * NB * BLK * 100,
            bytes_accessed=12 * 2**20,
            transcendentals=blocks * heads * BLK * NB * BLK,
        ),
        name="sums",
    )(umap, counts, bias_gain, edge_bias)


def attend_kernel(row_devs, gain_ref, q_ref, t_ref, m_ref, *rest):
    got, out_ref = rest[:row_devs], rest[row_devs]
    pair = pl.program_id(0)
    units = CAP * row_devs
    rows2 = q_ref.shape[1]
    first_k = lax.broadcasted_iota(jnp.int32, (CAP * BLK, 2 * HD), 1) < HD
    first = lax.broadcasted_iota(jnp.int32, (rows2, 2 * HD), 1) < HD

    def doubled(part, odd):
        rows = []
        for s in range(row_devs):
            x = got[s][part].astype(jnp.float32)
            y = swap_halves(x)
            low = jnp.where(first_k, y if odd else x, 0.0).astype(jnp.bfloat16)
            high = jnp.where(first_k, 0.0, x if odd else y).astype(jnp.bfloat16)
            for c in range(CAP):
                rows += [low[c * BLK : (c + 1) * BLK], high[c * BLK : (c + 1) * BLK]]
        return jnp.concatenate(rows, axis=0)

    def halves(x, op, fill):
        parts = [x[:, u * 2 * BLK : (u + 1) * 2 * BLK] for u in range(units)]
        while len(parts) > 1:
            parts = [op(parts[i], parts[i + 1]) for i in range(0, len(parts) - 1, 2)] + parts[len(parts) // 2 * 2 :]
        y = parts[0]
        reduce = jnp.max if op is jnp.maximum else jnp.sum
        low = reduce(jnp.where(first, y, fill), axis=1, keepdims=True)
        high = reduce(jnp.where(first, fill, y), axis=1, keepdims=True)
        return jnp.where(first, low, high)

    outs = []
    for odd in range(2):
        gain = gain_ref[2 * pair + odd] * LOG2E
        score = lax.dot_general(
            q_ref[odd], doubled(0, odd), (((1,), (1,)), ((), ())), preferred_element_type=jnp.float32
        )
        score = score * (HD**-0.5 * LOG2E) + m_ref[...].astype(jnp.float32) * gain
        top = halves(score, jnp.maximum, -jnp.inf)
        expo = jnp.exp2(score - jnp.concatenate([top] * units, axis=1)) * t_ref[odd].astype(jnp.float32)
        total = halves(expo, jnp.add, 0.0)
        mixed = jnp.dot(expo.astype(jnp.bfloat16), doubled(1, odd), preferred_element_type=jnp.float32)
        outs.append(mixed / total)
    a, b = outs
    out_ref[0] = jnp.where(first, a, swap_halves(b)).astype(jnp.bfloat16)
    out_ref[1] = jnp.where(first, swap_halves(a), b).astype(jnp.bfloat16)


def attend(bias_gain, q, t, m, got):
    heads, rows2, _ = q.shape
    wide = m.shape[1]
    row_devs = len(got)
    grid_spec = pltpu.PrefetchScalarGridSpec(
        num_scalar_prefetch=1,
        grid=(heads // 2,),
        in_specs=[
            pl.BlockSpec((2, rows2, 2 * HD), lambda p, *_: (p, 0, 0)),
            pl.BlockSpec((2, rows2, wide), lambda p, *_: (p, 0, 0)),
            pl.BlockSpec((rows2, wide), lambda p, *_: (0, 0)),
        ]
        + [pl.BlockSpec((2, CAP * BLK, 2 * HD), lambda p, *_: (0, 0, p))] * row_devs,
        out_specs=pl.BlockSpec((2, rows2, 2 * HD), lambda p, *_: (0, 0, p)),
    )
    return pl.pallas_call(
        functools.partial(attend_kernel, row_devs),
        out_shape=jax.ShapeDtypeStruct((2, rows2, heads * HD), jnp.bfloat16),
        grid_spec=grid_spec,
        compiler_params=pltpu.CompilerParams(vmem_limit_bytes=56 * 2**20),
        name="attend",
    )(bias_gain, q, t, m, *got)


def body(features, w_qkv, w_out, bias_gain, edge_bias, neighbours, counts):
    rows = features.shape[0]
    width = w_qkv.shape[2]
    blocks = rows // BLK
    row_devs = lax.axis_size("row")
    head_devs = lax.axis_size("head")
    me = lax.axis_index("row")
    z = lax.axis_index("head")
    units = CAP * row_devs

    owner, local = neighbours // blocks, neighbours % blocks
    hit = owner[None] == jnp.arange(row_devs, dtype=jnp.int32)[:, None, None]
    low = jnp.min(jnp.where(hit, local[None], blocks - 1), axis=(1, 2))
    high = jnp.max(jnp.where(hit, local[None], 0), axis=(1, 2))
    low_here = jnp.sum(jnp.where(hit, low[:, None, None], 0), axis=0)
    hop = lax.rem(owner - me + row_devs, row_devs)
    umap = CAP * hop + (local != low_here).astype(jnp.int32)
    wanted = jnp.stack([low, high], axis=1)
    requests = lax.all_to_all(wanted, "row", 0, 0, tiled=True)
    serve = lax.rem(me - jnp.arange(row_devs, dtype=jnp.int32) + row_devs, row_devs)
    requests = jnp.sum(
        jnp.where((serve[:, None] == jnp.arange(row_devs)[None])[:, :, None], requests[None], 0), axis=1
    ).astype(jnp.int32)

    columns = w_out.shape[1] // head_devs
    w_cols = []
    for s in range(head_devs):
        piece = lax.dynamic_slice_in_dim(w_out, lax.rem(z - s + head_devs, head_devs) * columns, columns, 1)
        if s:
            piece = lax.ppermute(piece, "head", [((d + s) % head_devs, d) for d in range(head_devs)])
        w_cols.append(piece)

    q, *sends = project(features, w_qkv, requests, row_devs)
    got = [
        lax.ppermute(x, "row", [((d + s) % row_devs, d) for d in range(row_devs)]) if s else x
        for s, x in enumerate(sends)
    ]
    got = [x.reshape(CAP * BLK, 2, width).transpose(1, 0, 2) for x in got]
    t, m = sums(umap, counts, bias_gain, edge_bias, units)
    mine = attend(bias_gain, q, t, m, got)
    total = None
    for s in range(head_devs):
        x = mine
        if s:
            x = lax.ppermute(x, "head", [((d + s) % head_devs, d) for d in range(head_devs)])
        part = jnp.einsum("arc,co->aro", x, w_cols[s], preferred_element_type=jnp.float32)
        total = part if total is None else total + part
    total = total.reshape(2, blocks, HALF, columns).transpose(1, 0, 2, 3)
    return total.reshape(rows, columns).astype(jnp.bfloat16)


def solution(mesh):
    in_specs = (
        P("row", None),
        P(None, None, "head"),
        P("head", None),
        P("head"),
        P("row", None, None),
        P("row", None),
        P("row"),
    )
    return jax.shard_map(body, mesh=mesh, in_specs=in_specs, out_specs=P("row", "head"), check_vma=False)
```

time: 381 us -> 109 us (0.29)
  the two profiles are of different devices: /device:TPU:0 before, /device:TPU:31 now
where the time goes in v1:
time: 109 us; the launch traced here: 108 us
  waiting for transfers between devices  35.1 us (32%)
  Pallas kernels  29.4 us (27%)
  starting transfers between devices  20.8 us (19%)
  local copies, waits for them, and re-layouts  18.5 us (17%)
  other arithmetic  2.1 us (2%)
  matrix products  1.88 us (2%)
    ppermute x3, waiting for transfers between devices, body(): lax.ppermute(x, 'head', [((d + s) % head_devs, d) for d in range(head_dev...  26.6 us
    pallas_call x1, Pallas kernels, sums(): pl.pallas_call(functools.partial(sums_kernel, heads, units), out_shape=[j...  18.7 us
    ppermute x7, starting transfers between devices, body(): lax.ppermute(x, 'row', [((d + s) % row_devs, d) for d in range(row_devs)])  11.5 us
    unnamed x18, local copies, waits for them, and re-layouts  9.77 us
    pallas_call x1, Pallas kernels, attend(): pl.pallas_call(functools.partial(attend_kernel, row_devs), out_shape=jax....  9.08 us
    reshape x8, local copies, waits for them, and re-layouts, body(): got = [x.reshape(CAP * BLK, 2, width).transpose(1, 0, 2) for x in got]  6.18 us
    ppermute x3, waiting for transfers between devices, body(): lax.ppermute(piece, 'head', [((d + s) % head_devs, d) for d in range(head...  5.11 us
    all_to_all x1, starting transfers between devices, body(): requests = lax.all_to_all(wanted, 'row', 0, 0, tiled=True)  4.51 us
  transfers between devices with their start and end apart: 14, of which 5 were waited for; matrix products, arithmetic and copies ran while one was open for 8% of the time, Pallas kernels for 17%

profile of v1, /device:TPU:31, one launch (start us, length us, event | category | flops | bytes accessed | tf_op | source)
XLA Modules:
  0.0 107.9 jit_solution(2796048257996482399)
XLA Ops:
  1.8 4.5 %all-to-all-start = ((s32[8,1,2]{2,1,0:T(1,128)}), s32[8,1,2]{2,1,0:T(1,128)S(1)}, u32[]{:S(2)}, u32[]{:S(2)}) async-start(s32[8,1,2]{2,1,0:T(1,128)} %copy.48), calls=%async_computation | async-start | bytes 8192 | tf_op jit(solution)/shard_map/all_to_all | solution.py:230
  6.5 1.7 %all-to-all-done = s32[8,1,2]{2,1,0:T(1,128)S(1)} async-done(((s32[8,1,2]{2,1,0:T(1,128)}), s32[8,1,2]{2,1,0:T(1,128)S(1)}, u32[]{:S(2)}, u32[]{:S(2)}) %all-to-all-start) | async-done | bytes 96 | tf_op jit(solution)/shard_map/all_to_all | solution.py:230
  8.5 1.4 %copy-done.1 = bf16[3,1024,256]{2,1,0:T(8,128)(2,1)S(1)} copy-done((bf16[3,1024,256]{2,1,0:T(8,128)(2,1)S(1)}, bf16[3,1024,256]{2,1,0:T(8,128)(2,1)}, u32[]{:S(2)}) %copy-start.1) | copy-done | bytes 1572888
  9.9 1.2 %copy-done.2 = bf16[512,1024]{1,0:T(8,128)(2,1)S(1)} copy-done((bf16[512,1024]{1,0:T(8,128)(2,1)S(1)}, bf16[512,1024]{1,0:T(8,128)(2,1)}, u32[]{:S(2)}) %copy-start.2) | copy-done | bytes 1048600
  11.1 1.6 %project.1 = (bf16[4,256,128]{2,1,0:T(8,128)(2,1)S(1)}, bf16[128,512]{1,0:T(8,128)(2,1)S(1)}, bf16[128,512]{1,0:T(8,128)(2,1)S(1)}, bf16[128,512]{1,0:T(8,128)(2...) custom-call(s32[8,2]{1,0:T(8,128)S(1)} %copy.50.req_ref, ...), custom_call_target="tpu_custom_call" | custom-call | tf_op jit(solution)/shard_map/project/pallas_call | solution.py:53
  13.5 1.8 %collective-permute-start.2 = (bf16[128,512]{1,0:T(8,128)(2,1)S(1)}, bf16[128,512]{1,0:T(8,128)(2,1)S(1)}, u32[]{:S(2)}, u32[]{:S(2)}) collective-permute-start(bf16[128,512]{1,0:T(8,128)(2,1)S(1)} %get-tuple-element.22), channel_id=1, source_target_pairs={{12,0},{16,4},{20,8},{24,12},{28,16},{0,20},{4,24},{8,28},{13,1},{... | collective-permute-start | bytes 393224 | tf_op jit(solution)/shard_map/ppermute | solution.py:246
  15.3 1.2 %collective-permute-start.3 = (bf16[128,512]{1,0:T(8,128)(2,1)S(1)}, bf16[128,512]{1,0:T(8,128)(2,1)S(1)}, u32[]{:S(2)}, u32[]{:S(2)}) collective-permute-start(bf16[128,512]{1,0:T(8,128)(2,1)S(1)} %get-tuple-element.23), channel_id=1, source_target_pairs={{16,0},{20,4},{24,8},{28,12},{0,16},{4,20},{8,24},{12,28},{17,1},{... | collective-permute-start | bytes 393224 | tf_op jit(solution)/shard_map/ppermute | solution.py:246
  17.4 1.2 %collective-permute-start.5 = (bf16[128,512]{1,0:T(8,128)(2,1)S(1)}, bf16[128,512]{1,0:T(8,128)(2,1)S(1)}, u32[]{:S(2)}, u32[]{:S(2)}) collective-permute-start(bf16[128,512]{1,0:T(8,128)(2,1)S(1)} %get-tuple-element.25), channel_id=1, source_target_pairs={{24,0},{28,4},{0,8},{4,12},{8,16},{12,20},{16,24},{20,28},{25,1},{... | collective-permute-start | bytes 393224 | tf_op jit(solution)/shard_map/ppermute | solution.py:246
  18.7 1.7 %collective-permute-start.6 = (bf16[128,512]{1,0:T(8,128)(2,1)S(1)}, bf16[128,512]{1,0:T(8,128)(2,1)S(1)}, u32[]{:S(2)}, u32[]{:S(2)}) collective-permute-start(bf16[128,512]{1,0:T(8,128)(2,1)S(1)} %get-tuple-element.26), channel_id=1, source_target_pairs={{28,0},{0,4},{4,8},{8,12},{12,16},{16,20},{20,24},{24,28},{29,1},{... | collective-permute-start | bytes 393224 | tf_op jit(solution)/shard_map/ppermute | solution.py:246
  20.4 1.6 %collective-permute-done.3 = bf16[128,512]{1,0:T(8,128)(2,1)S(1)} collective-permute-done((bf16[128,512]{1,0:T(8,128)(2,1)S(1)}, bf16[128,512]{1,0:T(8,128)(2,1)S(1)}, u32[]{:S(2)}, u32[]{:S(2)}) %collective-permute-start.3) | collective-permute-done | bytes 131104 | tf_op jit(solution)/shard_map/ppermute | solution.py:246
  22.0 5.3 %collective-permute-start.1 = (bf16[128,512]{1,0:T(8,128)(2,1)S(1)}, bf16[128,512]{1,0:T(8,128)(2,1)S(1)}, u32[]{:S(2)}, u32[]{:S(2)}) collective-permute-start(bf16[128,512]{1,0:T(8,128)(2,1)S(1)} %get-tuple-element.21), channel_id=1, source_target_pairs={{8,0},{12,4},{16,8},{20,12},{24,16},{28,20},{0,24},{4,28},{9,1},{1... | collective-permute-start | bytes 393224 | tf_op jit(solution)/shard_map/ppermute | solution.py:246
  28.0 2.2 %copy-done.6 = bf16[8,64,4096]{2,1,0:T(8,128)(2,1)S(1)} copy-done((bf16[8,64,4096]{2,1,0:T(8,128)(2,1)S(1)}, bf16[8,64,4096]{2,1,0:T(8,128)(2,1)}, u32[]{:S(2)}) %copy-start.6) | copy-done | bytes 4194328
  30.8 18.7 %sums.1 = (bf16[4,256,2048]{2,1,0:T(8,128)(2,1)S(1)}, bf16[256,2048]{1,0:T(8,128)(2,1)S(1)}) custom-call(s32[8,64]{1,0:T(8,128)S(1)} %fusion.11.umap_ref, s32[8]{0:T(128)S(1)} %copy-done.7, f32[4]{0:T(128)S(1)} %copy-done.5, bf16[8,64,4096]{2,1,0:T(8,128)(2,1)S(1)} %copy-done.6), custom_call_target="tpu_custom_call" | custom-call | flops 8388608000 | bytes 12582912 | tf_op jit(solution)/shard_map/sums/pallas_call | solution.py:125
  49.5 2.0 %copy-done = bf16[4,256,2048]{2,1,0:T(8,128)(2,1)} copy-done((bf16[4,256,2048]{2,1,0:T(8,128)(2,1)}, bf16[4,256,2048]{2,1,0:T(8,128)(2,1)S(1)}, u32[]{:S(2)}) %copy-start) | copy-done | bytes 4194328
  51.5 1.0 copy-done.3
  52.6 0.8 copy.52
  58.8 0.8 copy.56
  59.6 9.1 %attend.1 = bf16[2,256,256]{2,1,0:T(8,128)(2,1)} custom-call(f32[4]{0:T(128)} %gain_ref.3, bf16[4,256,128]{2,1,0:T(8,128)(2,1)} %copy-done.4, bf16[4,256,2048]{2,1,0:T(8,128)(2,1)} %copy-done, bf16[256,2048]{1,0:T(8,128)(2,1)} %copy-done.3, bf16[2,128,256]{2,1,0:T(8,128)(2,1)} %bitcast.42, bf16[2,128,256]{2,1,0:T(8,128)(2,1)} %bitcast.48, ...), custom_call_target="tpu_custom_call" | custom-call | tf_op jit(solution)/shard_map/attend/pallas_call | solution.py:203
  69.2 3.1 %collective-permute-start.12 = (bf16[256,256]{1,0:T(8,128)(2,1)S(1)}, bf16[256,256]{1,0:T(8,128)(2,1)S(1)}, u32[]{:S(2)}, u32[]{:S(2)}) collective-permute-start(bf16[256,256]{1,0:T(8,128)(2,1)S(1)} %get-tuple-element.31), channel_id=1, source_target_pairs={{3,0},{0,1},{1,2},{2,3},{7,4},{4,5},{5,6},{6,7},{11,8},{8,9},{9,10... | collective-permute-start | bytes 393224 | tf_op jit(solution)/shard_map/ppermute | solution.py:241
  72.4 1.2 %collective-permute-start.11 = (bf16[2,256,256]{2,1,0:T(8,128)(2,1)}, bf16[2,256,256]{2,1,0:T(8,128)(2,1)S(1)}, u32[]{:S(2)}, u32[]{:S(2)}) collective-permute-start(bf16[2,256,256]{2,1,0:T(8,128)(2,1)} %attend.1), channel_id=1, source_target_pairs={{3,0},{0,1},{1,2},{2,3},{7,4},{4,5},{5,6},{6,7},{11,8},{8,9},{9,10... | collective-permute-start | bytes 786440 | tf_op jit(solution)/shard_map/ppermute | solution.py:256
  73.5 1.2 %fusion.6 = f32[2,256,256]{2,1,0:T(8,128)S(1)} fusion(bf16[2,256,256]{2,1,0:T(8,128)(2,1)} %attend.1, bf16[256,1024]{1,0:T(8,128)(2,1)S(1)} %copy-done.8, s32[]{:T(128)S(6)} %select_n.45), kind=kOutput, calls=%fused_computation.8 | convolution fusion | flops 67108864 | bytes 917508 | tf_op jit(solution)/shard_map/arc,co->aro/dot_general | solution.py:257
  74.8 5.1 %collective-permute-done.8 = bf16[256,256]{1,0:T(8,128)(2,1)S(1)} collective-permute-done((bf16[256,256]{1,0:T(8,128)(2,1)S(1)}, bf16[256,256]{1,0:T(8,128)(2,1)S(1)}, u32[]{:S(2)}, u32[]{:S(2)}) %collective-permute-start.8) | collective-permute-done | bytes 131104 | tf_op jit(solution)/shard_map/ppermute | solution.py:241
  80.1 10.3 %collective-permute-done.11 = bf16[2,256,256]{2,1,0:T(8,128)(2,1)S(1)} collective-permute-done((bf16[2,256,256]{2,1,0:T(8,128)(2,1)}, bf16[2,256,256]{2,1,0:T(8,128)(2,1)S(1)}, u32[]{:S(2)}, u32[]{:S(2)}) %collective-permute-start.11) | collective-permute-done | bytes 262176 | tf_op jit(solution)/shard_map/ppermute | solution.py:256
  90.7 16.3 %collective-permute-done.9 = bf16[2,256,256]{2,1,0:T(8,128)(2,1)S(1)} collective-permute-done((bf16[2,256,256]{2,1,0:T(8,128)(2,1)}, bf16[2,256,256]{2,1,0:T(8,128)(2,1)S(1)}, u32[]{:S(2)}, u32[]{:S(2)}) %collective-permute-start.9) | collective-permute-done | bytes 262176 | tf_op jit(solution)/shard_map/ppermute | solution.py:256
  (58 shorter events, 12.8 us)
Async XLA Ops:
  1.8 6.4 %all-to-all-start = ((s32[8,1,2]{2,1,0:T(1,128)}), s32[8,1,2]{2,1,0:T(1,128)S(1)}, u32[]{:S(2)}, u32[]{:S(2)}) async-start(s32[8,1,2]{2,1,0:T(1,128)} %copy.48), calls=%async_computation | async-start | bytes 8192 | tf_op jit(solution)/shard_map/all_to_all | solution.py:230
  8.5 1.4 %copy-start.1 = (bf16[3,1024,256]{2,1,0:T(8,128)(2,1)S(1)}, bf16[3,1024,256]{2,1,0:T(8,128)(2,1)}, u32[]{:S(2)}) copy-start(bf16[3,1024,256]{2,1,0:T(8,128)(2,1)} %w_ref.1) | copy-start | bytes 4718596
  9.9 1.2 %copy-start.2 = (bf16[512,1024]{1,0:T(8,128)(2,1)S(1)}, bf16[512,1024]{1,0:T(8,128)(2,1)}, u32[]{:S(2)}) copy-start(bf16[512,1024]{1,0:T(8,128)(2,1)} %x_ref.1) | copy-start | bytes 3145732
  12.8 0.7 copy-start.4
  13.5 6.9 %collective-permute-start.2 = (bf16[128,512]{1,0:T(8,128)(2,1)S(1)}, bf16[128,512]{1,0:T(8,128)(2,1)S(1)}, u32[]{:S(2)}, u32[]{:S(2)}) collective-permute-start(bf16[128,512]{1,0:T(8,128)(2,1)S(1)} %get-tuple-element.22), channel_id=1, source_target_pairs={{12,0},{16,4},{20,8},{24,12},{28,16},{0,20},{4,24},{8,28},{13,1},{... | collective-permute-start | bytes 393224 | tf_op jit(solution)/shard_map/ppermute | solution.py:246
  15.3 6.8 %collective-permute-start.3 = (bf16[128,512]{1,0:T(8,128)(2,1)S(1)}, bf16[128,512]{1,0:T(8,128)(2,1)S(1)}, u32[]{:S(2)}, u32[]{:S(2)}) collective-permute-start(bf16[128,512]{1,0:T(8,128)(2,1)S(1)} %get-tuple-element.23), channel_id=1, source_target_pairs={{16,0},{20,4},{24,8},{28,12},{0,16},{4,20},{8,24},{12,28},{17,1},{... | collective-permute-start | bytes 393224 | tf_op jit(solution)/shard_map/ppermute | solution.py:246
  17.1 38.0 %collective-permute-start.4 = (bf16[128,512]{1,0:T(8,128)(2,1)S(1)}, bf16[128,512]{1,0:T(8,128)(2,1)S(1)}, u32[]{:S(2)}, u32[]{:S(2)}) collective-permute-start(bf16[128,512]{1,0:T(8,128)(2,1)S(1)} %get-tuple-element.24), channel_id=1, source_target_pairs={{20,0},{24,4},{28,8},{0,12},{4,16},{8,20},{12,24},{16,28},{21,1},{... | collective-permute-start | bytes 393224 | tf_op jit(solution)/shard_map/ppermute | solution.py:246
  17.4 38.6 %collective-permute-start.5 = (bf16[128,512]{1,0:T(8,128)(2,1)S(1)}, bf16[128,512]{1,0:T(8,128)(2,1)S(1)}, u32[]{:S(2)}, u32[]{:S(2)}) collective-permute-start(bf16[128,512]{1,0:T(8,128)(2,1)S(1)} %get-tuple-element.25), channel_id=1, source_target_pairs={{24,0},{28,4},{0,8},{4,12},{8,16},{12,20},{16,24},{20,28},{25,1},{... | collective-permute-start | bytes 393224 | tf_op jit(solution)/shard_map/ppermute | solution.py:246
  18.7 38.3 %collective-permute-start.6 = (bf16[128,512]{1,0:T(8,128)(2,1)S(1)}, bf16[128,512]{1,0:T(8,128)(2,1)S(1)}, u32[]{:S(2)}, u32[]{:S(2)}) collective-permute-start(bf16[128,512]{1,0:T(8,128)(2,1)S(1)} %get-tuple-element.26), channel_id=1, source_target_pairs={{28,0},{0,4},{4,8},{8,12},{12,16},{16,20},{20,24},{24,28},{29,1},{... | collective-permute-start | bytes 393224 | tf_op jit(solution)/shard_map/ppermute | solution.py:246
  20.4 37.4 %collective-permute-start = (bf16[128,512]{1,0:T(8,128)(2,1)S(1)}, bf16[128,512]{1,0:T(8,128)(2,1)S(1)}, u32[]{:S(2)}, u32[]{:S(2)}) collective-permute-start(bf16[128,512]{1,0:T(8,128)(2,1)S(1)} %get-tuple-element.20), channel_id=1, source_target_pairs={{4,0},{8,4},{12,8},{16,12},{20,16},{24,20},{28,24},{0,28},{5,1},{9... | collective-permute-start | bytes 393224 | tf_op jit(solution)/shard_map/ppermute | solution.py:246
  22.0 36.7 %collective-permute-start.1 = (bf16[128,512]{1,0:T(8,128)(2,1)S(1)}, bf16[128,512]{1,0:T(8,128)(2,1)S(1)}, u32[]{:S(2)}, u32[]{:S(2)}) collective-permute-start(bf16[128,512]{1,0:T(8,128)(2,1)S(1)} %get-tuple-element.21), channel_id=1, source_target_pairs={{8,0},{12,4},{16,8},{20,12},{24,16},{28,20},{0,24},{4,28},{9,1},{1... | collective-permute-start | bytes 393224 | tf_op jit(solution)/shard_map/ppermute | solution.py:246
  27.3 0.7 copy-start.5
  28.0 2.2 %copy-start.6 = (bf16[8,64,4096]{2,1,0:T(8,128)(2,1)S(1)}, bf16[8,64,4096]{2,1,0:T(8,128)(2,1)}, u32[]{:S(2)}) copy-start(bf16[8,64,4096]{2,1,0:T(8,128)(2,1)} %bias_ref.1) | copy-start | bytes 12582916
  30.2 0.7 copy-start.7
  49.5 2.0 %copy-start = (bf16[4,256,2048]{2,1,0:T(8,128)(2,1)}, bf16[4,256,2048]{2,1,0:T(8,128)(2,1)S(1)}, u32[]{:S(2)}) copy-start(bf16[4,256,2048]{2,1,0:T(8,128)(2,1)S(1)} %get-tuple-element.17.t_ref) | copy-start | bytes 12582916
  51.5 1.0 copy-start.3
  56.9 12.0 %copy-start.8 = (bf16[256,1024]{1,0:T(8,128)(2,1)S(1)}, bf16[256,1024]{1,0:T(8,128)(2,1)}, u32[]{:S(2)}) copy-start(bf16[256,1024]{1,0:T(8,128)(2,1)} %param.9) | copy-start | bytes 1572868
  68.7 11.2 %collective-permute-start.7 = (bf16[2,256,256]{2,1,0:T(8,128)(2,1)}, bf16[2,256,256]{2,1,0:T(8,128)(2,1)S(1)}, u32[]{:S(2)}, u32[]{:S(2)}) collective-permute-start(bf16[2,256,256]{2,1,0:T(8,128)(2,1)} %attend.1), channel_id=1, source_target_pairs={{1,0},{2,1},{3,2},{0,3},{5,4},{6,5},{7,6},{4,7},{9,8},{10,9},{11,1... | collective-permute-start | bytes 786440 | tf_op jit(solution)/shard_map/ppermute | solution.py:256
  68.9 10.9 %collective-permute-start.8 = (bf16[256,256]{1,0:T(8,128)(2,1)S(1)}, bf16[256,256]{1,0:T(8,128)(2,1)S(1)}, u32[]{:S(2)}, u32[]{:S(2)}) collective-permute-start(bf16[256,256]{1,0:T(8,128)(2,1)S(1)} %get-tuple-element.30), channel_id=1, source_target_pairs={{1,0},{2,1},{3,2},{0,3},{5,4},{6,5},{7,6},{4,7},{9,8},{10,9},{11,1... | collective-permute-start | bytes 393224 | tf_op jit(solution)/shard_map/ppermute | solution.py:241
  69.2 11.0 %collective-permute-start.12 = (bf16[256,256]{1,0:T(8,128)(2,1)S(1)}, bf16[256,256]{1,0:T(8,128)(2,1)S(1)}, u32[]{:S(2)}, u32[]{:S(2)}) collective-permute-start(bf16[256,256]{1,0:T(8,128)(2,1)S(1)} %get-tuple-element.31), channel_id=1, source_target_pairs={{3,0},{0,1},{1,2},{2,3},{7,4},{4,5},{5,6},{6,7},{11,8},{8,9},{9,10... | collective-permute-start | bytes 393224 | tf_op jit(solution)/shard_map/ppermute | solution.py:241
  72.2 18.4 %collective-permute-start.10 = (bf16[256,256]{1,0:T(8,128)(2,1)S(1)}, bf16[256,256]{1,0:T(8,128)(2,1)S(1)}, u32[]{:S(2)}, u32[]{:S(2)}) collective-permute-start(bf16[256,256]{1,0:T(8,128)(2,1)S(1)} %get-tuple-element.29), channel_id=1, source_target_pairs={{2,0},{3,1},{0,2},{1,3},{6,4},{7,5},{4,6},{5,7},{10,8},{11,9},{8,1... | collective-permute-start | bytes 393224 | tf_op jit(solution)/shard_map/ppermute | solution.py:241
  72.4 18.1 %collective-permute-start.11 = (bf16[2,256,256]{2,1,0:T(8,128)(2,1)}, bf16[2,256,256]{2,1,0:T(8,128)(2,1)S(1)}, u32[]{:S(2)}, u32[]{:S(2)}) collective-permute-start(bf16[2,256,256]{2,1,0:T(8,128)(2,1)} %attend.1), channel_id=1, source_target_pairs={{3,0},{0,1},{1,2},{2,3},{7,4},{4,5},{5,6},{6,7},{11,8},{8,9},{9,10... | collective-permute-start | bytes 786440 | tf_op jit(solution)/shard_map/ppermute | solution.py:256
  79.9 27.1 %collective-permute-start.9 = (bf16[2,256,256]{2,1,0:T(8,128)(2,1)}, bf16[2,256,256]{2,1,0:T(8,128)(2,1)S(1)}, u32[]{:S(2)}, u32[]{:S(2)}) collective-permute-start(bf16[2,256,256]{2,1,0:T(8,128)(2,1)} %attend.1), channel_id=1, source_target_pairs={{2,0},{3,1},{0,2},{1,3},{6,4},{7,5},{4,6},{5,7},{10,8},{11,9},{8,1... | collective-permute-start | bytes 786440 | tf_op jit(solution)/shard_map/ppermute | solution.py:256

commit v2 on v1

v2 whole, which is shorter than its diff:
```python
import functools

import jax
import jax.numpy as jnp
from jax import lax
from jax.experimental import pallas as pl
from jax.experimental.pallas import tpu as pltpu
from jax.sharding import PartitionSpec as P

HD = 64
BLK = 64
NB = 64
HALF = BLK // 2
CAP = 2
NEG = -1e30
LOG2E = 1.4426950408889634


def swap_halves(x):
    return pltpu.roll(x, HD, 1)


MESH = pl.DeviceIdType.MESH


def greet(peers):
    barrier = pltpu.get_barrier_semaphore()
    for peer in peers:
        pl.semaphore_signal(barrier, inc=1, device_id=peer, device_id_type=MESH)
    pl.semaphore_wait(barrier, len(peers))


def exchange_kernel(
    row_devs, head_devs, want_ref, x_hbm, w_hbm, wout_ref, q_ref, got_ref, wcol_ref,
    x_ref, w_ref, kv, reqs, sends, load_sem, req_send, req_recv, kv_send, kv_recv, w_send, w_recv,
):
    loads = [
        pltpu.make_async_copy(x_hbm, x_ref, load_sem.at[0]),
        pltpu.make_async_copy(w_hbm, w_ref, load_sem.at[1]),
    ]
    for load in loads:
        load.start()
    me, z = lax.axis_index("row"), lax.axis_index("head")
    rows, width = x_ref.shape[0], w_ref.shape[2]
    columns = wcol_ref.shape[2]

    def row_peer(s):
        return {"row": lax.rem(me + s + row_devs, row_devs)}

    def head_peer(s):
        return {"head": lax.rem(z + s + head_devs, head_devs)}

    greet([row_peer(s) for s in range(1, row_devs)] + [head_peer(s) for s in range(1, head_devs)])
    asks, moves = [None], [None]
    for s in range(1, row_devs):
        asks.append(
            pltpu.make_async_remote_copy(
                want_ref.at[s], reqs.at[s], req_send.at[s], req_recv.at[s], device_id=row_peer(s), device_id_type=MESH
            )
        )
        asks[s].start()
    for s in range(1, head_devs):
        at = pl.multiple_of(lax.rem(z - s + head_devs, head_devs) * columns, columns)
        moves.append(
            pltpu.make_async_remote_copy(
                wout_ref.at[:, pl.ds(at, columns)], wcol_ref.at[s], w_send.at[s], w_recv.at[s],
                device_id=head_peer(-s), device_id_type=MESH,
            )
        )
        moves[s].start()
    wcol_ref[0] = wout_ref[:, pl.ds(pl.multiple_of(z * columns, columns), columns)]

    for load in loads:
        load.wait()
    x = x_ref[...]
    for t in range(2):
        kv[t] = jnp.dot(x, w_ref[1 + t], preferred_element_type=jnp.float32).astype(jnp.bfloat16)

    column = lax.broadcasted_iota(jnp.int32, (BLK, rows), 1)
    row = lax.broadcasted_iota(jnp.int32, (BLK, rows), 0)

    def pick(ref, s, dst):
        for c in range(CAP):
            start = jnp.concatenate([ref[s, c : c + 1, :]] * (rows // 128), axis=1)
            hot = (column == start * BLK + row).astype(jnp.float32).astype(jnp.bfloat16)
            for t in range(2):
                dst[s, t, c * BLK : (c + 1) * BLK, :] = jnp.dot(
                    hot, kv[t], preferred_element_type=jnp.float32
                ).astype(jnp.bfloat16)

    copies = [None]
    for s in range(1, row_devs):
        asks[s].wait_recv()
        pick(reqs, s, sends)
        copies.append(
            pltpu.make_async_remote_copy(
                sends.at[s], got_ref.at[s], kv_send.at[s], kv_recv.at[s], device_id=row_peer(-s), device_id_type=MESH
            )
        )
        copies[s].start()
    pick(want_ref, 0, got_ref)

    q = jnp.dot(x, w_ref[0], preferred_element_type=jnp.float32).reshape(rows // BLK, 2, HALF, width)
    top = q[:, 0].reshape(rows // 2, width)
    bottom = q[:, 1].reshape(rows // 2, width)
    first = lax.broadcasted_iota(jnp.int32, (rows // 2, 2 * HD), 1) < HD
    for pair in range(width // (2 * HD)):
        a = top[:, pair * 2 * HD : (pair + 1) * 2 * HD]
        b = bottom[:, pair * 2 * HD : (pair + 1) * 2 * HD]
        q_ref[2 * pair] = jnp.where(first, a, swap_halves(b)).astype(jnp.bfloat16)
        q_ref[2 * pair + 1] = jnp.where(first, swap_halves(a), b).astype(jnp.bfloat16)

    for s in range(1, row_devs):
        asks[s].wait_send()
        copies[s].wait()
    for s in range(1, head_devs):
        moves[s].wait()


def exchange(want, features, w_qkv, w_out, row_devs, head_devs):
    rows, depth = features.shape
    width = w_qkv.shape[2]
    vmem = pl.BlockSpec(memory_space=pltpu.VMEM)
    anywhere = pl.BlockSpec(memory_space=pl.ANY)
    dma = pltpu.SemaphoreType.DMA
    return pl.pallas_call(
        functools.partial(exchange_kernel, row_devs, head_devs),
        out_shape=[
            jax.ShapeDtypeStruct((width // HD, rows // 2, 2 * HD), jnp.bfloat16),
            jax.ShapeDtypeStruct((row_devs, 2, CAP * BLK, width), jnp.bfloat16),
            jax.ShapeDtypeStruct((head_devs, w_out.shape[0], w_out.shape[1] // head_devs), jnp.bfloat16),
        ],
        in_specs=[vmem, anywhere, anywhere, vmem],
        out_specs=[vmem] * 3,
        scratch_shapes=[
            pltpu.VMEM((rows, depth), jnp.bfloat16),
            pltpu.VMEM(w_qkv.shape, jnp.bfloat16),
            pltpu.VMEM((2, rows, width), jnp.bfloat16),
            pltpu.VMEM((row_devs, 8, 128), jnp.int32),
            pltpu.VMEM((row_devs, 2, CAP * BLK, width), jnp.bfloat16),
            dma((2,)),
            dma((row_devs,)),
            dma((row_devs,)),
            dma((row_devs,)),
            dma((row_devs,)),
            dma((head_devs,)),
            dma((head_devs,)),
        ],
        compiler_params=pltpu.CompilerParams(
            vmem_limit_bytes=40 * 2**20, collective_id=0, has_side_effects=True
        ),
        name="exchange",
    )(want, features, w_qkv, w_out)


def sums_kernel(heads, units, umap_ref, count_ref, gain_ref, bias_ref, t_ref, m_ref, tiles, best, acc):
    g = pl.program_id(0)
    count = count_ref[g]
    best[...] = jnp.full(best.shape, NEG, jnp.float32)
    acc[...] = jnp.zeros(acc.shape, jnp.float32)
    first = lax.broadcasted_iota(jnp.int32, (HALF, 2 * BLK), 1) < BLK

    def arrange(i, carry):
        for step in range(2):
            pair = i * 2 + step
            at = pl.multiple_of(pair * 2 * BLK, 2 * BLK)
            a = bias_ref[0, 0:HALF, pl.ds(at, 2 * BLK)].astype(jnp.float32)
            b = bias_ref[0, HALF:BLK, pl.ds(at, 2 * BLK)].astype(jnp.float32)
            for odd in range(2):
                j = 2 * pair + odd
                tile = jnp.where(first, swap_halves(a), b) if odd else jnp.where(first, a, swap_halves(b))
                tile = jnp.where(j < count, tile, NEG)
                tiles[j] = tile
                u = umap_ref[g, j]
                best[u] = jnp.maximum(best[u], tile)
        return carry

    lax.fori_loop(0, NB // 4, arrange, 0)
    gains = [gain_ref[h] * LOG2E for h in range(heads)]

    def add(i, carry):
        for step in range(4):
            j = i * 4 + step
            u = umap_ref[g, j]
            d = tiles[j] - best[u]
            e = [jnp.exp2(d * gains[h]) for h in range(heads)]
            for h in range(heads):
                acc[u, h] += e[h]
        return carry

    lax.fori_loop(0, (count + 3) // 4, add, 0)
    for u in range(units):
        m_ref[:, u * 2 * BLK : (u + 1) * 2 * BLK] = best[u].astype(jnp.bfloat16)
        for h in range(heads):
            t_ref[h, :, u * 2 * BLK : (u + 1) * 2 * BLK] = acc[u, h].astype(jnp.bfloat16)


def sums(umap, counts, bias_gain, edge_bias, units):
    blocks = umap.shape[0]
    heads = bias_gain.shape[0]
    wide = units * 2 * BLK
    rows2 = blocks * HALF
    grid_spec = pltpu.PrefetchScalarGridSpec(
        num_scalar_prefetch=3,
        grid=(blocks,),
        in_specs=[pl.BlockSpec((1, BLK, NB * BLK), lambda g, *_: (g, 0, 0))],
        out_specs=[
            pl.BlockSpec((heads, HALF, wide), lambda g, *_: (0, g, 0)),
            pl.BlockSpec((HALF, wide), lambda g, *_: (g, 0)),
        ],
        scratch_shapes=[
            pltpu.VMEM((NB, HALF, 2 * BLK), jnp.float32),
            pltpu.VMEM((units, HALF, 2 * BLK), jnp.float32),
            pltpu.VMEM((units, heads, HALF, 2 * BLK), jnp.float32),
        ],
    )
    return pl.pallas_call(
        functools.partial(sums_kernel, heads, units),
        out_shape=[
            jax.ShapeDtypeStruct((heads, rows2, wide), jnp.bfloat16),
            jax.ShapeDtypeStruct((rows2, wide), jnp.bfloat16),
        ],
        grid_spec=grid_spec,
        compiler_params=pltpu.CompilerParams(vmem_limit_bytes=40 * 2**20),
        cost_estimate=pl.CostEstimate(
            flops=10 * blocks * heads * BLK * NB * BLK * 100,
            bytes_accessed=12 * 2**20,
            transcendentals=blocks * heads * BLK * NB * BLK,
        ),
        name="sums",
    )(umap, counts, bias_gain, edge_bias)


def attend_kernel(
    row_devs, head_devs, gain_ref, q_ref, t_ref, m_ref, got_ref, wcol_ref, out_ref, att, send_sem, recv_sem
):
    z = lax.axis_index("head")
    peers = [{"head": lax.rem(z + s, head_devs)} for s in range(head_devs)]
    greet(peers[1:])
    units = CAP * row_devs
    rows2 = q_ref.shape[1]
    first_k = lax.broadcasted_iota(jnp.int32, (CAP * BLK, 2 * HD), 1) < HD
    first = lax.broadcasted_iota(jnp.int32, (rows2, 2 * HD), 1) < HD

    def doubled(part, pair, odd):
        rows = []
        for s in range(row_devs):
            x = got_ref[s, part, :, pair * 2 * HD : (pair + 1) * 2 * HD].astype(jnp.float32)
            y = swap_halves(x)
            low = jnp.where(first_k, y if odd else x, 0.0).astype(jnp.bfloat16)
            high = jnp.where(first_k, 0.0, x if odd else y).astype(jnp.bfloat16)
            for c in range(CAP):
                rows += [low[c * BLK : (c + 1) * BLK], high[c * BLK : (c + 1) * BLK]]
        return jnp.concatenate(rows, axis=0)

    def halves(x, op, fill):
        parts = [x[:, u * 2 * BLK : (u + 1) * 2 * BLK] for u in range(units)]
        while len(parts) > 1:
            parts = [op(parts[i], parts[i + 1]) for i in range(0, len(parts) - 1, 2)] + parts[len(parts) // 2 * 2 :]
        y = parts[0]
        reduce = jnp.max if op is jnp.maximum else jnp.sum
        low = reduce(jnp.where(first, y, fill), axis=1, keepdims=True)
        high = reduce(jnp.where(first, fill, y), axis=1, keepdims=True)
        return jnp.where(first, low, high)

    copies = []
    for pair in range(q_ref.shape[0] // 2):
        outs = []
        for odd in range(2):
            h = 2 * pair + odd
            gain = gain_ref[h] * LOG2E
            score = lax.dot_general(
                q_ref[h], doubled(0, pair, odd), (((1,), (1,)), ((), ())), preferred_element_type=jnp.float32
            )
            score = score * (HD**-0.5 * LOG2E) + m_ref[...].astype(jnp.float32) * gain
            top = halves(score, jnp.maximum, -jnp.inf)
            expo = jnp.exp2(score - jnp.concatenate([top] * units, axis=1)) * t_ref[h].astype(jnp.float32)
            total = halves(expo, jnp.add, 0.0)
            mixed = jnp.dot(expo.astype(jnp.bfloat16), doubled(1, pair, odd), preferred_element_type=jnp.float32)
            outs.append(mixed / total)
        a, b = outs
        lanes = slice(pair * 2 * HD, (pair + 1) * 2 * HD)
        att[0, 0, :, lanes] = jnp.where(first, a, swap_halves(b)).astype(jnp.bfloat16)
        att[0, 1, :, lanes] = jnp.where(first, swap_halves(a), b).astype(jnp.bfloat16)
        for s in range(1, head_devs):
            here = pl.ds(pair * 2 * HD, 2 * HD)
            copy = pltpu.make_async_remote_copy(
                att.at[0, :, :, here],
                att.at[s, :, :, here],
                send_sem.at[pair, s],
                recv_sem.at[pair, s],
                device_id=peers[head_devs - s],
                device_id_type=MESH,
            )
            copy.start()
            copies.append((s, copy))
    blocks, columns = out_ref.shape[0], out_ref.shape[3]
    total = [None, None]
    for s in range(head_devs):
        for shift, copy in copies:
            if shift == s:
                copy.wait_recv()
        for side in range(2):
            part = jnp.dot(att[s, side], wcol_ref[s], preferred_element_type=jnp.float32)
            total[side] = part if s == 0 else total[side] + part
    for side in range(2):
        out_ref[:, side] = total[side].reshape(blocks, HALF, columns).astype(jnp.bfloat16)
    for _, copy in copies:
        copy.wait_send()


def attend(bias_gain, q, t, m, got, wcol):
    heads, rows2, _ = q.shape
    head_devs, _, columns = wcol.shape
    vmem = pl.BlockSpec(memory_space=pltpu.VMEM)
    return pl.pallas_call(
        functools.partial(attend_kernel, got.shape[0], head_devs),
        out_shape=jax.ShapeDtypeStruct((rows2 // HALF, 2, HALF, columns), jnp.bfloat16),
        in_specs=[pl.BlockSpec(memory_space=pltpu.SMEM)] + [vmem] * 5,
        out_specs=vmem,
        scratch_shapes=[
            pltpu.VMEM((head_devs, 2, rows2, heads * HD), jnp.bfloat16),
            pltpu.SemaphoreType.DMA((heads // 2, head_devs)),
            pltpu.SemaphoreType.DMA((heads // 2, head_devs)),
        ],
        compiler_params=pltpu.CompilerParams(
            vmem_limit_bytes=56 * 2**20, collective_id=1, has_side_effects=True
        ),
        name="attend",
    )(bias_gain, q, t, m, got, wcol)


def body(features, w_qkv, w_out, bias_gain, edge_bias, neighbours, counts):
    rows = features.shape[0]
    blocks = rows // BLK
    row_devs = lax.axis_size("row")
    head_devs = lax.axis_size("head")
    me = lax.axis_index("row")
    units = CAP * row_devs

    owner, local = neighbours // blocks, neighbours % blocks
    hop = lax.rem(owner - me + row_devs, row_devs)
    hit = hop[None] == jnp.arange(row_devs, dtype=jnp.int32)[:, None, None]
    low = jnp.min(jnp.where(hit, local[None], blocks - 1), axis=(1, 2))
    high = jnp.max(jnp.where(hit, local[None], 0), axis=(1, 2))
    low_here = jnp.sum(jnp.where(hit, low[:, None, None], 0), axis=0)
    umap = CAP * hop + (local != low_here).astype(jnp.int32)
    wanted = jnp.stack([low, high], axis=1)
    want = jnp.broadcast_to(jnp.pad(wanted, ((0, 0), (0, 6)))[:, :, None], (row_devs, 8, 128))
    q, got, wcol = exchange(want, features, w_qkv, w_out, row_devs, head_devs)
    t, m = sums(umap, counts, bias_gain, edge_bias, units)
    out = attend(bias_gain, q, t, m, got, wcol)
    return out.reshape(rows, out.shape[3])


def solution(mesh):
    in_specs = (
        P("row", None),
        P(None, None, "head"),
        P("head", None),
        P("head"),
        P("row", None, None),
        P("row", None),
        P("row"),
    )
    return jax.shard_map(body, mesh=mesh, in_specs=in_specs, out_specs=P("row", "head"), check_vma=False)
```

time: 109 us -> 89.5 us (0.82)
  the two profiles are of different devices: /device:TPU:31 before, /device:TPU:0 now
where the time goes in v2:
time: 89.5 us; the launch traced here: 89 us
  Pallas kernels  72.6 us (81%)
  local copies, waits for them, and re-layouts  14.4 us (16%)
  other arithmetic  1.88 us (2%)
    pallas_call x1, Pallas kernels, attend(): pl.pallas_call(functools.partial(attend_kernel, got.shape[0], head_devs),...  33.1 us
    pallas_call x1, Pallas kernels, exchange(): pl.pallas_call(functools.partial(exchange_kernel, row_devs, head_devs), o...  23 us
    pallas_call x1, Pallas kernels, sums(): pl.pallas_call(functools.partial(sums_kernel, heads, units), out_shape=[j...  16.5 us
    unnamed x24, local copies, waits for them, and re-layouts  14.3 us

profile of v2, /device:TPU:0, one launch (start us, length us, event | category | flops | bytes accessed | tf_op | source)
XLA Modules:
  0.0 89.0 jit_solution(16696881708282990726)
XLA Ops:
  0.0 0.7 negate_select_fusion
  0.7 0.4 select_reduce_fusion.2
  1.1 0.1 copy.10
  1.2 0.1 select_reduce_fusion
  1.3 0.7 convert_add_fusion.umap_ref
  2.0 0.1 broadcast_in_dim.42.want_ref
  2.0 0.0 copy-start.1
  2.0 1.4 %copy-done.1 = bf16[3,1024,256]{2,1,0:T(8,128)(2,1)S(1)} copy-done((bf16[3,1024,256]{2,1,0:T(8,128)(2,1)S(1)}, bf16[3,1024,256]{2,1,0:T(8,128)(2,1)}, u32[]{:S(2)}) %copy-start.1) | copy-done | bytes 1572888
  3.5 1.2 %copy-done.2 = bf16[512,1024]{1,0:T(8,128)(2,1)S(1)} copy-done((bf16[512,1024]{1,0:T(8,128)(2,1)S(1)}, bf16[512,1024]{1,0:T(8,128)(2,1)}, u32[]{:S(2)}) %copy-start.2) | copy-done | bytes 1048600
  4.7 1.0 %copy-done.5 = bf16[256,1024]{1,0:T(8,128)(2,1)S(1)} copy-done((bf16[256,1024]{1,0:T(8,128)(2,1)S(1)}, bf16[256,1024]{1,0:T(8,128)(2,1)}, u32[]{:S(2)}) %copy-start.5) | copy-done | bytes 524312
  5.7 23.0 %exchange.1 = (bf16[4,256,128]{2,1,0:T(8,128)(2,1)S(1)}, bf16[8,2,128,256]{3,2,1,0:T(8,128)(2,1)S(1)}, bf16[4,256,256]{2,1,0:T(8,128)(2,1)S(1)}) custom-call(s32[8,8,128]{2,1,0:T(8,128)S(1)} %broadcast_in_dim.42.want_ref, bf16[512,1024]{1,0:T(8,128)(2,1)S(1)} %copy-done.2, bf16[3,1024,256]{2,1,0:T(8,128)(2,1)S(1)} %copy-done.1, bf16[256,1024]{1,0:T(8,128)(2,1)S(1)} %copy-done.5), custom_call_target="tpu_custom_call" | custom-call | tf_op jit(solution)/shard_map/exchange/pallas_call | solution.py:126
  28.8 0.0 copy-start.3
  28.8 1.0 %copy-done.3 = bf16[8,2,128,256]{3,2,1,0:T(8,128)(2,1)} copy-done((bf16[8,2,128,256]{3,2,1,0:T(8,128)(2,1)}, bf16[8,2,128,256]{3,2,1,0:T(8,128)(2,1)S(1)}, u32[]{:S(2)}) %copy-start.3) | copy-done | bytes 1048600
  29.8 0.8 copy-done.6
  30.6 0.7 copy-done.7
  31.3 0.7 copy-done.8
  31.9 2.2 %copy-done.9 = bf16[8,64,4096]{2,1,0:T(8,128)(2,1)S(1)} copy-done((bf16[8,64,4096]{2,1,0:T(8,128)(2,1)S(1)}, bf16[8,64,4096]{2,1,0:T(8,128)(2,1)}, u32[]{:S(2)}) %copy-start.9) | copy-done | bytes 4194328
  34.1 0.7 copy-done.10
  34.8 16.5 %sums.1 = (bf16[4,256,2048]{2,1,0:T(8,128)(2,1)S(1)}, bf16[256,2048]{1,0:T(8,128)(2,1)S(1)}) custom-call(s32[8,64]{1,0:T(8,128)S(1)} %convert_add_fusion.umap_ref, s32[8]{0:T(128)S(1)} %copy-done.10, f32[4]{0:T(128)S(1)} %copy-done.8, bf16[8,64,4096]{2,1,0:T(8,128)(2,1)S(1)} %copy-done.9), custom_call_target="tpu_custom_call" | custom-call | flops 8388608000 | bytes 12582912 | tf_op jit(solution)/shard_map/sums/pallas_call | solution.py:217
  51.3 0.0 copy-start
  51.3 1.9 %copy-done = bf16[4,256,2048]{2,1,0:T(8,128)(2,1)} copy-done((bf16[4,256,2048]{2,1,0:T(8,128)(2,1)}, bf16[4,256,2048]{2,1,0:T(8,128)(2,1)S(1)}, u32[]{:S(2)}) %copy-start) | copy-done | bytes 4194328
  53.2 1.0 %copy-done.4 = bf16[256,2048]{1,0:T(8,128)(2,1)} copy-done((bf16[256,2048]{1,0:T(8,128)(2,1)}, bf16[256,2048]{1,0:T(8,128)(2,1)S(1)}, u32[]{:S(2)}) %copy-start.4) | copy-done | bytes 1048600
  54.2 33.1 %attend.1 = bf16[8,2,32,256]{3,2,1,0:T(8,128)(2,1)} custom-call(f32[4]{0:T(128)} %gain_ref.3, bf16[4,256,128]{2,1,0:T(8,128)(2,1)} %copy-done.7, bf16[4,256,2048]{2,1,0:T(8,128)(2,1)} %copy-done, bf16[256,2048]{1,0:T(8,128)(2,1)} %copy-done.4, bf16[8,2,128,256]{3,2,1,0:T(8,128)(2,1)} %copy-done.3, bf16[4,256,256]{2,1,0:T(8,128)(2,1)} %copy-done.6), custom_call_target="tpu_custom_call" | custom-call | tf_op jit(solution)/shard_map/attend/pallas_call | solution.py:316
  87.3 1.7 %copy.12 = bf16[512,256]{1,0:T(8,128)(2,1)} copy(bf16[512,256]{1,0:T(8,128)(2,1)} %bitcast.3) | data formatting | bytes 524288
  (10 shorter events, 0.0 us)
Async XLA Ops:
  2.0 1.4 %copy-start.1 = (bf16[3,1024,256]{2,1,0:T(8,128)(2,1)S(1)}, bf16[3,1024,256]{2,1,0:T(8,128)(2,1)}, u32[]{:S(2)}) copy-start(bf16[3,1024,256]{2,1,0:T(8,128)(2,1)} %w_hbm.1) | copy-start | bytes 4718596
  3.5 1.2 %copy-start.2 = (bf16[512,1024]{1,0:T(8,128)(2,1)S(1)}, bf16[512,1024]{1,0:T(8,128)(2,1)}, u32[]{:S(2)}) copy-start(bf16[512,1024]{1,0:T(8,128)(2,1)} %x_hbm.1) | copy-start | bytes 3145732
  4.7 1.0 %copy-start.5 = (bf16[256,1024]{1,0:T(8,128)(2,1)S(1)}, bf16[256,1024]{1,0:T(8,128)(2,1)}, u32[]{:S(2)}) copy-start(bf16[256,1024]{1,0:T(8,128)(2,1)} %wout_ref.1) | copy-start | bytes 1572868
  28.8 1.0 %copy-start.3 = (bf16[8,2,128,256]{3,2,1,0:T(8,128)(2,1)}, bf16[8,2,128,256]{3,2,1,0:T(8,128)(2,1)S(1)}, u32[]{:S(2)}) copy-start(bf16[8,2,128,256]{3,2,1,0:T(8,128)(2,1)S(1)} %get-tuple-element.13.got_ref) | copy-start | bytes 3145732
  29.8 0.8 copy-start.6
  30.6 0.7 copy-start.7
  31.3 0.7 copy-start.8
  31.9 2.2 %copy-start.9 = (bf16[8,64,4096]{2,1,0:T(8,128)(2,1)S(1)}, bf16[8,64,4096]{2,1,0:T(8,128)(2,1)}, u32[]{:S(2)}) copy-start(bf16[8,64,4096]{2,1,0:T(8,128)(2,1)} %bias_ref.1) | copy-start | bytes 12582916
  34.1 0.7 copy-start.10
  51.3 1.9 %copy-start = (bf16[4,256,2048]{2,1,0:T(8,128)(2,1)}, bf16[4,256,2048]{2,1,0:T(8,128)(2,1)S(1)}, u32[]{:S(2)}) copy-start(bf16[4,256,2048]{2,1,0:T(8,128)(2,1)S(1)} %get-tuple-element.11.t_ref) | copy-start | bytes 12582916
  53.2 1.0 %copy-start.4 = (bf16[256,2048]{1,0:T(8,128)(2,1)}, bf16[256,2048]{1,0:T(8,128)(2,1)S(1)}, u32[]{:S(2)}) copy-start(bf16[256,2048]{1,0:T(8,128)(2,1)S(1)} %get-tuple-element.12.m_ref) | copy-start | bytes 3145732

commit v3 on v2

--- a/solution.py
+++ b/solution.py
@@ -121,7 +121,7 @@
     rows, depth = features.shape
     width = w_qkv.shape[2]
     vmem = pl.BlockSpec(memory_space=pltpu.VMEM)
-    anywhere = pl.BlockSpec(memory_space=pl.ANY)
+    anywhere = pl.BlockSpec(memory_space=pltpu.HBM)
     dma = pltpu.SemaphoreType.DMA
     return pl.pallas_call(
         functools.partial(exchange_kernel, row_devs, head_devs),
@@ -147,7 +147,7 @@
             dma((head_devs,)),
         ],
         compiler_params=pltpu.CompilerParams(
-            vmem_limit_bytes=40 * 2**20, collective_id=0, has_side_effects=True
+            vmem_limit_bytes=60 * 2**20, collective_id=0, has_side_effects=True
         ),
         name="exchange",
     )(want, features, w_qkv, w_out)
@@ -221,7 +221,7 @@
             jax.ShapeDtypeStruct((rows2, wide), jnp.bfloat16),
         ],
         grid_spec=grid_spec,
-        compiler_params=pltpu.CompilerParams(vmem_limit_bytes=40 * 2**20),
+        compiler_params=pltpu.CompilerParams(vmem_limit_bytes=60 * 2**20),
         cost_estimate=pl.CostEstimate(
             flops=10 * blocks * heads * BLK * NB * BLK * 100,
             bytes_accessed=12 * 2**20,
@@ -324,7 +324,7 @@
             pltpu.SemaphoreType.DMA((heads // 2, head_devs)),
         ],
         compiler_params=pltpu.CompilerParams(
-            vmem_limit_bytes=56 * 2**20, collective_id=1, has_side_effects=True
+            vmem_limit_bytes=60 * 2**20, collective_id=1, has_side_effects=True
         ),
         name="attend",
     )(bias_gain, q, t, m, got, wcol)

time: 89.5 us -> 82.4 us (0.921)
  local copies, waits for them, and re-layouts: 14.4 us -> 2.45 us
  Pallas kernels: 72.6 us -> 77.2 us
    unnamed x24 -> x2, local copies, waits for them, and re-layouts: 14.3 us -> 1.75 us
    pallas_call x1, Pallas kernels: 16.5 us -> 22.4 us  [sums(): pl.pallas_call(functools.partial(sums_kernel, heads, units), out_shape=[j...]
    pallas_call x1, Pallas kernels: 33.1 us -> 29.7 us  [attend(): pl.pallas_call(functools.partial(attend_kernel, got.shape[0], head_devs),...]
    pallas_call x1, Pallas kernels: 23 us -> 25.1 us  [exchange(): pl.pallas_call(functools.partial(exchange_kernel, row_devs, head_devs), o...]
where the time goes in v3:
time: 82.4 us; the launch traced here: 82.1 us
  Pallas kernels  77.2 us (94%)
  other arithmetic  2.47 us (3%)
  local copies, waits for them, and re-layouts  2.45 us (3%)
    pallas_call x1, Pallas kernels, attend(): pl.pallas_call(functools.partial(attend_kernel, got.shape[0], head_devs),...  29.7 us
    pallas_call x1, Pallas kernels, exchange(): pl.pallas_call(functools.partial(exchange_kernel, row_devs, head_devs), o...  25.1 us
    pallas_call x1, Pallas kernels, sums(): pl.pallas_call(functools.partial(sums_kernel, heads, units), out_shape=[j...  22.4 us
    unnamed x2, local copies, waits for them, and re-layouts  1.75 us

profile of v3, /device:TPU:0, one launch (start us, length us, event | category | flops | bytes accessed | tf_op | source)
XLA Modules:
  0.0 82.1 jit_solution(16229695475175202686)
XLA Ops:
  0.0 0.7 negate_select_fusion
  0.7 0.4 select_reduce_fusion.2
  1.1 0.1 copy.10
  1.2 0.1 select_reduce_fusion
  1.3 1.3 %convert_add_fusion.umap_ref = s32[8,64]{1,0:T(8,128)} fusion(s32[8,64]{1,0:T(8,128)S(1)} %get-tuple-element.17, s32[8,64]{1,0:T(8,128)S(1)} %select_reduce_fusion, s32[8,64]{1,0:T(8,128)} %param.12), kind=kLoop, calls=%fused_computation.14 | loop fusion | flops 7680 | bytes 8192 | tf_op jit(solution)/shard_map/add | solution.py:347
  2.6 0.7 broadcast_in_dim.42.want_ref
  3.3 25.1 %exchange.1 = (bf16[4,256,128]{2,1,0:T(8,128)(2,1)}, bf16[8,2,128,256]{3,2,1,0:T(8,128)(2,1)}, bf16[4,256,256]{2,1,0:T(8,128)(2,1)}) custom-call(s32[8,8,128]{2,1,0:T(8,128)} %broadcast_in_dim.42.want_ref, bf16[512,1024]{1,0:T(8,128)(2,1)} %x_hbm.1, bf16[3,1024,256]{2,1,0:T(8,128)(2,1)} %w_hbm.1, bf16[256,1024]{1,0:T(8,128)(2,1)} %wout_ref.1), custom_call_target="tpu_custom_call" | custom-call | tf_op jit(solution)/shard_map/exchange/pallas_call | solution.py:126
  28.3 22.4 %sums.1 = (bf16[4,256,2048]{2,1,0:T(8,128)(2,1)}, bf16[256,2048]{1,0:T(8,128)(2,1)}) custom-call(s32[8,64]{1,0:T(8,128)} %convert_add_fusion.umap_ref, s32[8]{0:T(128)} %count_ref.1, f32[4]{0:T(128)} %gain_ref.3, bf16[8,64,4096]{2,1,0:T(8,128)(2,1)} %bias_ref.1), custom_call_target="tpu_custom_call" | custom-call | flops 8388608000 | bytes 12582912 | tf_op jit(solution)/shard_map/sums/pallas_call | solution.py:217
  50.8 29.7 %attend.1 = bf16[8,2,32,256]{3,2,1,0:T(8,128)(2,1)} custom-call(f32[4]{0:T(128)} %gain_ref.3, bf16[4,256,128]{2,1,0:T(8,128)(2,1)} %get-tuple-element.10.q_ref, bf16[4,256,2048]{2,1,0:T(8,128)(2,1)} %get-tuple-element.11.t_ref, bf16[256,2048]{1,0:T(8,128)(2,1)} %get-tuple-element.12.m_ref, bf16[8,2,128,256]{3,2,1,0:T(8,128)(2,1)} %get-tuple-element.13.got_ref, ...), custom_call_target="tpu_custom_call" | custom-call | tf_op jit(solution)/shard_map/attend/pallas_call | solution.py:316
  80.5 1.7 %copy.12 = bf16[512,256]{1,0:T(8,128)(2,1)} copy(bf16[512,256]{1,0:T(8,128)(2,1)} %bitcast.3) | data formatting | bytes 524288
  (2 shorter events, 0.0 us)

commit v4 on v3

--- a/solution.py
+++ b/solution.py
@@ -161,8 +161,8 @@
     first = lax.broadcasted_iota(jnp.int32, (HALF, 2 * BLK), 1) < BLK
 
     def arrange(i, carry):
-        for step in range(2):
-            pair = i * 2 + step
+        for step in range(4):
+            pair = i * 4 + step
             at = pl.multiple_of(pair * 2 * BLK, 2 * BLK)
             a = bias_ref[0, 0:HALF, pl.ds(at, 2 * BLK)].astype(jnp.float32)
             b = bias_ref[0, HALF:BLK, pl.ds(at, 2 * BLK)].astype(jnp.float32)
@@ -175,12 +175,12 @@
                 best[u] = jnp.maximum(best[u], tile)
         return carry
 
-    lax.fori_loop(0, NB // 4, arrange, 0)
+    lax.fori_loop(0, NB // 8, arrange, 0)
     gains = [gain_ref[h] * LOG2E for h in range(heads)]
 
     def add(i, carry):
-        for step in range(4):
-            j = i * 4 + step
+        for step in range(8):
+            j = i * 8 + step
             u = umap_ref[g, j]
             d = tiles[j] - best[u]
             e = [jnp.exp2(d * gains[h]) for h in range(heads)]
@@ -188,7 +188,7 @@
                 acc[u, h] += e[h]
         return carry
 
-    lax.fori_loop(0, (count + 3) // 4, add, 0)
+    lax.fori_loop(0, (count + 7) // 8, add, 0)
     for u in range(units):
         m_ref[:, u * 2 * BLK : (u + 1) * 2 * BLK] = best[u].astype(jnp.bfloat16)
         for h in range(heads):

time: 82.4 us -> 78.3 us (0.950)
  Pallas kernels: 77.2 us -> 73.2 us
    pallas_call x1, Pallas kernels: 22.4 us -> 14.9 us  [sums(): pl.pallas_call(functools.partial(sums_kernel, heads, units), out_shape=[j...]
    pallas_call x1, Pallas kernels: 29.7 us -> 33.2 us  [attend(): pl.pallas_call(functools.partial(attend_kernel, got.shape[0], head_devs),...]
where the time goes in v4:
time: 78.3 us; the launch traced here: 78.2 us
  Pallas kernels  73.2 us (93%)
  other arithmetic  2.47 us (3%)
  local copies, waits for them, and re-layouts  2.45 us (3%)
    pallas_call x1, Pallas kernels, attend(): pl.pallas_call(functools.partial(attend_kernel, got.shape[0], head_devs),...  33.2 us
    pallas_call x1, Pallas kernels, exchange(): pl.pallas_call(functools.partial(exchange_kernel, row_devs, head_devs), o...  25.1 us
    pallas_call x1, Pallas kernels, sums(): pl.pallas_call(functools.partial(sums_kernel, heads, units), out_shape=[j...  14.9 us
    unnamed x2, local copies, waits for them, and re-layouts  1.75 us

profile of v4, /device:TPU:0, one launch (start us, length us, event | category | flops | bytes accessed | tf_op | source)
XLA Modules:
  0.0 78.2 jit_solution(8804221017415775448)
XLA Ops:
  0.0 0.7 negate_select_fusion
  0.7 0.4 select_reduce_fusion.2
  1.1 0.1 copy.10
  1.2 0.1 select_reduce_fusion
  1.3 1.3 %convert_add_fusion.umap_ref = s32[8,64]{1,0:T(8,128)} fusion(s32[8,64]{1,0:T(8,128)S(1)} %get-tuple-element.17, s32[8,64]{1,0:T(8,128)S(1)} %select_reduce_fusion, s32[8,64]{1,0:T(8,128)} %param.12), kind=kLoop, calls=%fused_computation.14 | loop fusion | flops 7680 | bytes 8192 | tf_op jit(solution)/shard_map/add | solution.py:347
  2.6 0.7 broadcast_in_dim.42.want_ref
  3.3 25.1 %exchange.1 = (bf16[4,256,128]{2,1,0:T(8,128)(2,1)}, bf16[8,2,128,256]{3,2,1,0:T(8,128)(2,1)}, bf16[4,256,256]{2,1,0:T(8,128)(2,1)}) custom-call(s32[8,8,128]{2,1,0:T(8,128)} %broadcast_in_dim.42.want_ref, bf16[512,1024]{1,0:T(8,128)(2,1)} %x_hbm.1, bf16[3,1024,256]{2,1,0:T(8,128)(2,1)} %w_hbm.1, bf16[256,1024]{1,0:T(8,128)(2,1)} %wout_ref.1), custom_call_target="tpu_custom_call" | custom-call | tf_op jit(solution)/shard_map/exchange/pallas_call | solution.py:126
  28.3 14.9 %sums.1 = (bf16[4,256,2048]{2,1,0:T(8,128)(2,1)}, bf16[256,2048]{1,0:T(8,128)(2,1)}) custom-call(s32[8,64]{1,0:T(8,128)} %convert_add_fusion.umap_ref, s32[8]{0:T(128)} %count_ref.1, f32[4]{0:T(128)} %gain_ref.3, bf16[8,64,4096]{2,1,0:T(8,128)(2,1)} %bias_ref.1), custom_call_target="tpu_custom_call" | custom-call | flops 8388608000 | bytes 12582912 | tf_op jit(solution)/shard_map/sums/pallas_call | solution.py:217
  43.3 33.2 %attend.1 = bf16[8,2,32,256]{3,2,1,0:T(8,128)(2,1)} custom-call(f32[4]{0:T(128)} %gain_ref.3, bf16[4,256,128]{2,1,0:T(8,128)(2,1)} %get-tuple-element.10.q_ref, bf16[4,256,2048]{2,1,0:T(8,128)(2,1)} %get-tuple-element.11.t_ref, bf16[256,2048]{1,0:T(8,128)(2,1)} %get-tuple-element.12.m_ref, bf16[8,2,128,256]{3,2,1,0:T(8,128)(2,1)} %get-tuple-element.13.got_ref, ...), custom_call_target="tpu_custom_call" | custom-call | tf_op jit(solution)/shard_map/attend/pallas_call | solution.py:316
  76.5 1.7 %copy.12 = bf16[512,256]{1,0:T(8,128)(2,1)} copy(bf16[512,256]{1,0:T(8,128)(2,1)} %bitcast.3) | data formatting | bytes 524288
  (2 shorter events, 0.0 us)
